TPU v7x, 512 devices: a whole 4x8x8 slice. The times are simulated.
512 devices in a mesh: seq: 128 (over x, y_hi, z), head: 4 (over y_lo, core).
Axes of the slice: x: 4, y: 8 (y_hi: 4, y_lo: 2; y = y_hi * 2 + y_lo), z: 8, core: 2. Of those that a mesh axis runs over, the one named last changes fastest.
Arguments:
- queries: bfloat16 [32768, 16, 128], P('seq', 'head'), may hold values from -4.5 to 4.5
- keys: bfloat16 [32768, 16, 128], P('seq', 'head'), may hold values from -4.5 to 4.5
- values: bfloat16 [32768, 16, 128], P('seq', 'head'), may hold values from -6 to 6
- out_weight: bfloat16 [2048, 2048], P('head'), may hold values from -0.75 to 0.75
- cotangent: bfloat16 [32768, 2048], P(('seq', 'head')), may hold values from -6 to 6
- doc_lengths: int32 [128], replicated, may hold values from 1 to 1024, 32768 in all
Outputs:
- projected: bfloat16 [32768, 2048], P(('seq', 'head'))
- grad_queries: bfloat16 [32768, 16, 128], P('seq', 'head')
- grad_keys: bfloat16 [32768, 16, 128], P('seq', 'head')
- grad_values: bfloat16 [32768, 16, 128], P('seq', 'head')
Inputs may be any that keep to these rules, and one draw needn't show every extreme that they name: `doc_lengths`: lengths of the packed documents in order; they sum to 32768 and the longest is exactly 1024.
All inputs are finite; a program needn't handle non-finite values.
Results may differ from a plain program's by a relative error of at most 0.024.
Values may be sent and summed in bfloat16 or wider, within the bound.
A program may use at most 64 MiB of HBM per device.

v0:
```python
from functools import partial

import jax
import jax.numpy as jnp
from jax import lax
from jax.sharding import PartitionSpec as P

SPAN = 4


NEG = -1e30


def shifted(value, axis, steps):
    count = lax.axis_size(axis)
    leading, last = (max(0, -steps), min(count, count - steps))
    return lax.ppermute(value, axis, [(source, source + steps) for source in range(leading, last)])


def per_device(queries, keys, values, out_weight, cotangent, doc_lengths):
    tok_rows, head_count, head_size = queries.shape
    factor = float(head_size) ** (-0.5)
    center = lax.axis_index("seq")
    doc_ends = jnp.cumsum(doc_lengths)

    def block_docs(block_id):
        positions = block_id * tok_rows + jnp.arange(tok_rows, dtype=jnp.int32)
        members = jnp.sum((doc_ends[None, :] <= positions[:, None]).astype(jnp.int32), axis=1)
        return (positions, members)

    def scored(q_part, k_part, q_info, k_info):
        visible = (k_info[0][None, :] >= 0) & (k_info[0][None, :] <= q_info[0][:, None])
        visible = visible & (q_info[1][:, None] == k_info[1][None, :])
        product = (
            jnp.einsum("qgd,kgd->gqk", q_part, k_part, preferred_element_type=jnp.float32) * factor
        )
        return jnp.where(visible[None], product, NEG)

    own_info = block_docs(center)
    paired = jnp.stack([keys, values])

    def attend(running, kv_block, k_info):
        row_top, row_total, weighted = running
        raw_scores = scored(queries, kv_block[0], own_info, k_info)
        new_top = jnp.maximum(row_top, jnp.max(raw_scores, axis=-1))
        shrink = jnp.exp(row_top - new_top)
        prob_rows = jnp.exp(raw_scores - new_top[..., None])
        row_total = row_total * shrink + jnp.sum(prob_rows, axis=-1)
        weighted = weighted * shrink[..., None] + jnp.einsum(
            "gqk,kgd->gqd",
            prob_rows.astype(jnp.bfloat16),
            kv_block[1],
            preferred_element_type=jnp.float32,
        )
        return (new_top, row_total, weighted)

    running = (
        jnp.full((head_count, tok_rows), NEG, jnp.float32),
        jnp.zeros((head_count, tok_rows), jnp.float32),
        jnp.zeros((head_count, tok_rows, head_size), jnp.float32),
    )
    running = attend(running, paired, own_info)
    moving = paired
    stored = []
    for offset in range(1, SPAN + 1):
        moving = shifted(moving, "seq", 1)
        stored.append(moving)
        k_info = block_docs(center - offset)
        running = attend(running, moving, k_info)
    row_top, row_total, weighted = running
    attended = jnp.transpose(weighted / row_total[..., None], (1, 0, 2)).astype(jnp.bfloat16)
    logsum = row_top + jnp.log(row_total)
    flat_heads = attended.reshape(tok_rows, head_count * head_size)
    projected = lax.psum_scatter(
        jnp.dot(flat_heads, out_weight, preferred_element_type=jnp.float32).astype(jnp.bfloat16),
        "head",
        scatter_dimension=0,
        tiled=True,
    )
    d_flat = jnp.einsum(
        "te,he->th",
        lax.all_gather(cotangent, "head", axis=0, tiled=True),
        out_weight,
        preferred_element_type=jnp.float32,
    )
    d_attended = d_flat.astype(jnp.bfloat16).reshape(tok_rows, head_count, head_size)
    deltas = jnp.transpose(
        jnp.sum(d_attended.astype(jnp.float32) * attended.astype(jnp.float32), axis=-1)
    )

    def pair_grads(q_part, grad_part, lse_part, delta_part, q_info, k_part, v_part, k_info):
        raw_scores = scored(q_part, k_part, q_info, k_info)
        prob_rows = jnp.exp(raw_scores - lse_part[..., None])
        grad_v = jnp.einsum(
            "gqk,qgd->kgd",
            prob_rows.astype(jnp.bfloat16),
            grad_part,
            preferred_element_type=jnp.float32,
        )
        grad_probs = jnp.einsum(
            "qgd,kgd->gqk", grad_part, v_part, preferred_element_type=jnp.float32
        )
        grad_scores = (prob_rows * (grad_probs - delta_part[..., None])).astype(jnp.bfloat16)
        grad_q = jnp.einsum("gqk,kgd->qgd", grad_scores, k_part, preferred_element_type=jnp.float32)
        grad_k = jnp.einsum("gqk,qgd->kgd", grad_scores, q_part, preferred_element_type=jnp.float32)
        return (grad_q, grad_k, grad_v)

    sum_q, sum_k, sum_v = pair_grads(
        queries, d_attended, logsum, deltas, own_info, keys, values, own_info
    )
    moving = paired
    for offset in range(1, SPAN + 1):
        moving = shifted(moving, "seq", 1)
        compute = partial(
            pair_grads,
            queries,
            d_attended,
            logsum,
            deltas,
            own_info,
            moving[0],
            moving[1],
            block_docs(center - offset),
        )
        part_q, part_k, part_v = compute()
        sum_q = sum_q + part_q
        returned = shifted(jnp.stack([part_k, part_v]).astype(jnp.bfloat16), "seq", -offset).astype(
            jnp.float32
        )
        sum_k = sum_k + returned[0]
        sum_v = sum_v + returned[1]
    grad_queries = (sum_q * factor).astype(jnp.bfloat16)
    grad_keys = (sum_k * factor).astype(jnp.bfloat16)
    grad_values = sum_v.astype(jnp.bfloat16)
    return (projected, grad_queries, grad_keys, grad_values)


def solution(mesh):
    placed = (
        P("seq", "head", None),
        P("seq", "head", None),
        P("seq", "head", None),
        P("head", None),
        P(("seq", "head"), None),
        P(),
    )
    return jax.shard_map(
        per_device,
        mesh=mesh,
        in_specs=placed,
        out_specs=(
            P(("seq", "head"), None),
            P("seq", "head", None),
            P("seq", "head", None),
            P("seq", "head", None),
        ),
        check_vma=False,
    )
```

profile of v0, /device:TPU:30, one launch (start us, length us, event | category | flops | bytes accessed | tf_op | source)
XLA Modules:
  0.0 280.3 jit_solution(3993510717142571379)
XLA Ops:
  7.3 0.7 all-gather.2.cloned.1.call-update
  8.0 1.1 copy_bitcast_fusion
  9.1 0.8 pad_maximum_fusion
  9.9 4.3 %collective-permute-start = (bf16[2,256,4,128]{3,1,2,0:T(8,128)(2,1)}, bf16[2,256,4,128]{3,1,2,0:T(8,128)(2,1)S(1)}, u32[]{:S(2)}, u32[]{:S(2)}) collective-permute-start(bf16[2,256,4,128]{3,1,2,0:T(8,128)(2,1)} %pad_maximum_fusion), channel_id=1, source_target_pairs={{0,4},{4,8},{8,12},{12,16},{16,20},{20,24},{24,28},{28,32},{32,36}... | collective-permute-start | bytes 1572872 | tf_op jit(solution)/shard_map/ppermute | solution.py:17
  14.7 0.5 convert_reduce_fusion
  15.2 40.1 %collective-permute-done = bf16[2,256,4,128]{3,1,2,0:T(8,128)(2,1)S(1)} collective-permute-done((bf16[2,256,4,128]{3,1,2,0:T(8,128)(2,1)}, bf16[2,256,4,128]{3,1,2,0:T(8,128)(2,1)S(1)}, u32[]{:S(2)}, u32[]{:S(2)}) %collective-permute-start) | collective-permute-done | bytes 524320 | tf_op jit(solution)/shard_map/ppermute | solution.py:17
  55.3 1.9 collective-permute-start.1
  57.2 0.7 compare_and_fusion.2
  58.0 1.3 fusion.124
  59.3 36.0 %collective-permute-done.1 = bf16[2,256,4,128]{3,1,2,0:T(8,128)(2,1)S(1)} collective-permute-done((bf16[2,256,4,128]{3,1,2,0:T(8,128)(2,1)S(1)}, bf16[2,256,4,128]{3,1,2,0:T(8,128)(2,1)S(1)}, u32[]{:S(2)}, u32[]{:S(2)}) %collective-permute-start.1) | collective-permute-done | bytes 524320 | tf_op jit(solution)/shard_map/ppermute | solution.py:17
  95.2 1.9 collective-permute-start.2
  97.2 1.3 fusion.123
  98.5 1.3 fusion.122
  99.8 14.4 %collective-permute-done.2 = bf16[2,256,4,128]{3,1,2,0:T(8,128)(2,1)} collective-permute-done((bf16[2,256,4,128]{3,1,2,0:T(8,128)(2,1)S(1)}, bf16[2,256,4,128]{3,1,2,0:T(8,128)(2,1)}, u32[]{:S(2)}, u32[]{:S(2)}) %collective-permute-start.2) | collective-permute-done | bytes 524320 | tf_op jit(solution)/shard_map/ppermute | solution.py:17
  114.2 1.9 collective-permute-start.3
  116.1 2.3 fusion.121
  118.4 2.7 convolution_convert_fusion.9
  121.0 1.1 copy.158
  122.1 10.2 %collective-permute-done.3 = bf16[2,256,4,128]{3,1,2,0:T(8,128)(2,1)} collective-permute-done((bf16[2,256,4,128]{3,1,2,0:T(8,128)(2,1)}, bf16[2,256,4,128]{3,1,2,0:T(8,128)(2,1)}, u32[]{:S(2)}, u32[]{:S(2)}) %collective-permute-start.3) | collective-permute-done | bytes 524320 | tf_op jit(solution)/shard_map/ppermute | solution.py:17
  132.3 1.4 fusion.120
  133.8 1.4 fusion.44
  135.9 0.3 fusion.37
  136.2 0.3 fusion.39
  136.6 0.3 fusion.41
  136.9 0.3 fusion.43
  137.5 0.3 fusion.33
  138.0 0.3 fusion.20
  138.6 0.3 fusion.22
  138.9 1.3 fusion.24
  140.2 1.3 multiply_reduce_fusion
  141.5 1.2 fusion.18
  142.8 0.3 fusion.42
  143.1 1.2 fusion.17
  144.4 0.3 fusion.40
  144.7 0.3 fusion.16
  145.3 0.3 fusion.15
  145.6 0.3 fusion.36
  145.9 0.9 pad_maximum_fusion.1
  146.7 1.9 collective-permute-start.4
  148.7 0.9 pad_maximum_fusion.2
  149.5 1.9 collective-permute-start.5
  151.4 0.9 pad_maximum_fusion.3
  152.3 1.9 collective-permute-start.6
  154.2 0.9 pad_maximum_fusion.4
  155.1 2.1 collective-permute-start.7
  157.2 1.8 convolution_convert_fusion
  159.0 1.3 fusion.14
  160.4 0.3 convolution_bitcast_fusion.7
  160.8 0.3 fusion.27
  161.1 0.3 copy-done.13
  161.6 0.3 fusion.28
  162.0 1.3 fusion.29
  163.3 1.3 fusion.34
  164.6 0.9 copy.199
  165.5 10.2 %collective-permute-done.4 = bf16[2,256,4,128]{3,1,2,0:T(8,128)(2,1)} collective-permute-done((bf16[2,256,4,128]{3,1,2,0:T(8,128)(2,1)}, bf16[2,256,4,128]{3,1,2,0:T(8,128)(2,1)}, u32[]{:S(2)}, u32[]{:S(2)}) %collective-permute-start.4) | collective-permute-done | bytes 524320 | tf_op jit(solution)/shard_map/ppermute | solution.py:17
  175.7 1.1 convert_element_type.126
  176.8 90.8 %collective-permute-done.5 = bf16[2,256,4,128]{3,1,2,0:T(8,128)(2,1)} collective-permute-done((bf16[2,256,4,128]{3,1,2,0:T(8,128)(2,1)}, bf16[2,256,4,128]{3,1,2,0:T(8,128)(2,1)}, u32[]{:S(2)}, u32[]{:S(2)}) %collective-permute-start.5) | collective-permute-done | bytes 524320 | tf_op jit(solution)/shard_map/ppermute | solution.py:17
  267.6 1.1 convert_element_type.128
  268.8 1.1 convert_element_type.130
  269.9 1.1 convert_element_type.132
  271.0 0.3 fusion.76
  271.3 0.9 copy.200
  272.2 0.3 fusion.70
  272.5 0.9 copy.201
  (75 shorter events, 2.5 us)
Async XLA Ops:
  7.2 111.2 %copy-start = (bf16[512,2048]{1,0:T(8,128)(2,1)S(1)}, bf16[512,2048]{1,0:T(8,128)(2,1)}, u32[]{:S(2)}) copy-start(bf16[512,2048]{1,0:T(8,128)(2,1)} %param.9) | copy-start | bytes 6291460
  7.2 50.8 %copy-start.23 = (bf16[256,4,128]{2,1,0:T(4,128)(2,1)S(1)}, bf16[256,4,128]{2,1,0:T(4,128)(2,1)}, u32[]{:S(2)}) copy-start(bf16[256,4,128]{2,1,0:T(4,128)(2,1)} %param.7) | copy-start | bytes 786436
  7.2 7.1 %copy-start.25 = (s32[128]{0:T(128)S(1)}, s32[128]{0:T(128)}, u32[]{:S(2)}) copy-start(s32[128]{0:T(128)} %param.11) | copy-start | bytes 1540
  7.2 50.8 %copy-start.5 = (bf16[256,4,128]{2,1,0:T(4,128)(2,1)S(1)}, bf16[256,4,128]{2,1,0:T(4,128)(2,1)}, u32[]{:S(2)}) copy-start(bf16[256,4,128]{2,1,0:T(4,128)(2,1)} %param.6) | copy-start | bytes 786436
  7.2 111.1 %all-gather.2.cloned.1.call-start = ((), (), s32[]{:S(2)}) async-start(), calls=%async_computation.2 | async-start | bytes 1310720 | tf_op jit(solution)/shard_map/all_gather | solution.py:82
  7.9 265.5 %reduce-scatter.2.cloned.1.call-start = ((), (), s32[]{:S(2)}) async-start(), calls=%async_computation.1 | async-start | bytes 1310720 | tf_op jit(solution)/shard_map/reduce_scatter | solution.py:74
  9.9 45.3 %collective-permute-start = (bf16[2,256,4,128]{3,1,2,0:T(8,128)(2,1)}, bf16[2,256,4,128]{3,1,2,0:T(8,128)(2,1)S(1)}, u32[]{:S(2)}, u32[]{:S(2)}) collective-permute-start(bf16[2,256,4,128]{3,1,2,0:T(8,128)(2,1)} %pad_maximum_fusion), channel_id=1, source_target_pairs={{0,4},{4,8},{8,12},{12,16},{16,20},{20,24},{24,28},{28,32},{32,36}... | collective-permute-start | bytes 1572872 | tf_op jit(solution)/shard_map/ppermute | solution.py:17
  55.3 41.9 %copy-start.17 = (bf16[2,256,4,128]{3,1,2,0:T(8,128)(2,1)}, bf16[2,256,4,128]{3,1,2,0:T(8,128)(2,1)S(1)}, u32[]{:S(2)}) copy-start(bf16[2,256,4,128]{3,1,2,0:T(8,128)(2,1)S(1)} %collective-permute-done) | copy-start | bytes 1572868
  55.3 40.0 %collective-permute-start.1 = (bf16[2,256,4,128]{3,1,2,0:T(8,128)(2,1)S(1)}, bf16[2,256,4,128]{3,1,2,0:T(8,128)(2,1)S(1)}, u32[]{:S(2)}, u32[]{:S(2)}) collective-permute-start(bf16[2,256,4,128]{3,1,2,0:T(8,128)(2,1)S(1)} %collective-permute-done), channel_id=1, source_target_pairs={{0,4},{4,8},{8,12},{12,16},{16,20},{20,24},{24,28},{28,32},{32,36}... | collective-permute-start | bytes 1572872 | tf_op jit(solution)/shard_map/ppermute | solution.py:17
  95.2 3.2 %copy-start.20 = (bf16[2,256,4,128]{3,1,2,0:T(8,128)(2,1)}, bf16[2,256,4,128]{3,1,2,0:T(8,128)(2,1)S(1)}, u32[]{:S(2)}) copy-start(bf16[2,256,4,128]{3,1,2,0:T(8,128)(2,1)S(1)} %collective-permute-done.1) | copy-start | bytes 1572868
  95.2 18.9 %collective-permute-start.2 = (bf16[2,256,4,128]{3,1,2,0:T(8,128)(2,1)S(1)}, bf16[2,256,4,128]{3,1,2,0:T(8,128)(2,1)}, u32[]{:S(2)}, u32[]{:S(2)}) collective-permute-start(bf16[2,256,4,128]{3,1,2,0:T(8,128)(2,1)S(1)} %collective-permute-done.1), channel_id=1, source_target_pairs={{0,4},{4,8},{8,12},{12,16},{16,20},{20,24},{24,28},{28,32},{32,36}... | collective-permute-start | bytes 1572872 | tf_op jit(solution)/shard_map/ppermute | solution.py:17
  114.2 18.1 %collective-permute-start.3 = (bf16[2,256,4,128]{3,1,2,0:T(8,128)(2,1)}, bf16[2,256,4,128]{3,1,2,0:T(8,128)(2,1)}, u32[]{:S(2)}, u32[]{:S(2)}) collective-permute-start(bf16[2,256,4,128]{3,1,2,0:T(8,128)(2,1)} %collective-permute-done.2), channel_id=1, source_target_pairs={{0,4},{4,8},{8,12},{12,16},{16,20},{20,24},{24,28},{28,32},{32,36}... | collective-permute-start | bytes 1572872 | tf_op jit(solution)/shard_map/ppermute | solution.py:17
  122.1 13.2 %copy-start.2 = (f32[4,256,256]{1,2,0:T(8,128)S(1)}, f32[4,256,256]{1,2,0:T(8,128)}, u32[]{:S(2)}) copy-start(f32[4,256,256]{1,2,0:T(8,128)} %get-tuple-element.40) | copy-start | bytes 3145732
  132.3 3.2 %copy-start.1 = (f32[4,256,256]{1,2,0:T(8,128)S(1)}, f32[4,256,256]{1,2,0:T(8,128)}, u32[]{:S(2)}) copy-start(f32[4,256,256]{1,2,0:T(8,128)} %get-tuple-element.42) | copy-start | bytes 3145732
  136.2 1.2 copy-start.3
  136.2 1.3 copy-start.16
  136.9 1.1 copy-start.18
  137.5 1.1 copy-start.21
  140.2 2.6 copy-start.6
  142.8 1.9 copy-start.8
  144.4 0.9 copy-start.10
  145.0 0.9 copy-start.12
  145.6 6.7 %copy-start.14 = (bf16[4,256,256]{1,2,0:T(8,128)(2,1)}, bf16[4,256,256]{1,2,0:T(8,128)(2,1)S(1)}, u32[]{:S(2)}) copy-start(bf16[4,256,256]{1,2,0:T(8,128)(2,1)S(1)} %fusion.15) | copy-start | bytes 1572868
  146.7 28.9 %collective-permute-start.4 = (bf16[2,256,4,128]{3,1,2,0:T(8,128)(2,1)}, bf16[2,256,4,128]{3,1,2,0:T(8,128)(2,1)}, u32[]{:S(2)}, u32[]{:S(2)}) collective-permute-start(bf16[2,256,4,128]{3,1,2,0:T(8,128)(2,1)} %pad_maximum_fusion.1), channel_id=1, source_target_pairs={{4,0},{8,4},{12,8},{16,12},{20,16},{24,20},{28,24},{32,28},{36,32}... | collective-permute-start | bytes 1572872 | tf_op jit(solution)/shard_map/ppermute | solution.py:17
  149.5 118.1 %collective-permute-start.5 = (bf16[2,256,4,128]{3,1,2,0:T(8,128)(2,1)}, bf16[2,256,4,128]{3,1,2,0:T(8,128)(2,1)}, u32[]{:S(2)}, u32[]{:S(2)}) collective-permute-start(bf16[2,256,4,128]{3,1,2,0:T(8,128)(2,1)} %pad_maximum_fusion.2), channel_id=1, source_target_pairs={{8,0},{12,4},{16,8},{20,12},{24,16},{28,20},{32,24},{36,28},{40,32... | collective-permute-start | bytes 1572872 | tf_op jit(solution)/shard_map/ppermute | solution.py:17
  152.3 116.5 %collective-permute-start.6 = (bf16[2,256,4,128]{3,1,2,0:T(8,128)(2,1)}, bf16[2,256,4,128]{3,1,2,0:T(8,128)(2,1)}, u32[]{:S(2)}, u32[]{:S(2)}) collective-permute-start(bf16[2,256,4,128]{3,1,2,0:T(8,128)(2,1)} %pad_maximum_fusion.3), channel_id=1, source_target_pairs={{12,0},{16,4},{20,8},{24,12},{28,16},{32,20},{36,24},{40,28},{44,3... | collective-permute-start | bytes 1572872 | tf_op jit(solution)/shard_map/ppermute | solution.py:17
  155.1 114.8 %collective-permute-start.7 = (bf16[2,256,4,128]{3,1,2,0:T(8,128)(2,1)}, bf16[2,256,4,128]{3,1,2,0:T(8,128)(2,1)}, u32[]{:S(2)}, u32[]{:S(2)}) collective-permute-start(bf16[2,256,4,128]{3,1,2,0:T(8,128)(2,1)} %pad_maximum_fusion.4), channel_id=1, source_target_pairs={{16,0},{20,4},{24,8},{28,12},{32,16},{36,20},{40,24},{44,28},{48,3... | collective-permute-start | bytes 1572872 | tf_op jit(solution)/shard_map/ppermute | solution.py:17
  157.2 1.8 copy-start.4
  159.0 1.4 copy-start.24
  159.0 1.8 copy-start.15
  159.0 1.8 copy-start.19
  160.4 1.0 copy-start.13
  160.4 1.2 copy-start.22
  160.8 1.2 copy-start.11
  161.6 1.7 copy-start.9
  176.8 94.2 %copy-start.7 = (bf16[256,4,128]{2,1,0:T(4,128)(2,1)S(1)}, bf16[256,4,128]{2,1,0:T(4,128)(2,1)}, u32[]{:S(2)}) copy-start(bf16[256,4,128]{2,1,0:T(4,128)(2,1)} %param.6) | copy-start | bytes 786436
Sparse Core Ops, SparseCore 0:
  10.1 29.9 all-gather.1
  159.1 53.4 reduce-scatter.1
where the time goes:
time: 281 us; the launch traced here: 280 us
  waiting for transfers between devices  202 us (72%)
  matrix products  26.6 us (9%)
  starting transfers between devices  17.9 us (6%)
  between operations  14.8 us (5%)
  other arithmetic  12.3 us (4%)
  local copies, waits for them, and re-layouts  6.28 us (2%)
    ppermute x8, waiting for transfers between devices, shifted(): lax.ppermute(value, axis, [(source, source + steps) for source in range(l...  202 us
    ppermute x8, starting transfers between devices, shifted(): lax.ppermute(value, axis, [(source, source + steps) for source in range(l...  17.8 us
    dot_general x5, matrix products, scored(): jnp.einsum('qgd,kgd->gqk', q_part, k_part, preferred_element_type=jnp.flo...  7.58 us
  transfers between devices with their start and end apart: 10, of which 6 were waited for; matrix products, arithmetic and copies ran while one was open for 11% of the time, Pallas kernels for 0%

commit v1 on v0

v1 whole, which is shorter than its diff:
```python
import functools
import math

import jax
import jax.numpy as jnp
from jax import lax
from jax.experimental import pallas as pl
from jax.experimental.pallas import tpu as pltpu
from jax.sharding import PartitionSpec as P

MESH = pl.DeviceIdType.MESH
T = 256
HD = 128
NB = 4
RING = 8
WIN = 5
D = 2048
ROWS = 64
NEG = -1e30
FACTOR = HD ** (-0.5)
SCALE = FACTOR * math.log2(math.e)
BF = jnp.bfloat16
F32 = jnp.float32


def nt(a, b):
    return lax.dot_general(a, b, (((1,), (1,)), ((), ())), preferred_element_type=F32)


def nn(a, b):
    return jnp.dot(a, b, preferred_element_type=F32)


def fold(x, op):
    parts = [x[r : r + 8] for r in range(0, x.shape[0], 8)]
    while len(parts) > 1:
        parts = [
            op(parts[j], parts[j + 1]) if j + 1 < len(parts) else parts[j]
            for j in range(0, len(parts), 2)
        ]
    return parts[0]


def kernel(
    seq_size,
    q_ref,
    k_ref,
    v_ref,
    w_hbm,
    cot_ref,
    len_ref,
    proj_ref,
    dq_ref,
    dk_ref,
    dv_ref,
    kbuf,
    vbuf,
    qbuf,
    dobuf,
    kT,
    vT,
    cotbuf,
    wbuf,
    doloc,
    sbuf,
    pbuf,
    oT,
    linv,
    lo,
    dkacc,
    dvacc,
    hko,
    hvo,
    hki,
    hvi,
    oout,
    dqout,
    dkout,
    dvout,
    oin,
    pa_out,
    pa_in,
    pb_out,
    pb_in,
    in_send,
    in_recv,
    halo_send,
    halo_recv,
    cot_send,
    cot_recv,
    out_send,
    out_recv,
    hg_send,
    hg_recv,
    pr_send,
    pr_recv,
    w_sem,
):
    s = lax.axis_index("seq")
    h = lax.axis_index("head")
    z = lax.rem(s, RING)
    base = s - z
    c = lax.rem(h, 2)
    yl = h // 2
    half = z // NB
    zi = lax.rem(z, NB)
    sib = (s, h + 1 - 2 * c)
    across = (s, lax.rem(h + 2, 4))
    h_next = (lax.rem(s + RING * c, seq_size), h + 1 - 2 * c)
    h_prev = (lax.rem(s + seq_size - RING * (1 - c), seq_size), h + 1 - 2 * c)
    ring_adj = (lax.rem(s + seq_size + RING * (2 * c - 1), seq_size), h + 1 - 2 * c)

    def peer(i):
        return (base + NB * c + i, h - c + half)

    def is_self(i):
        return (c == half) & (zi == i)

    barrier = pltpu.get_barrier_semaphore()
    for dev in (sib, across, ring_adj):
        pl.semaphore_signal(barrier, inc=1, device_id=dev, device_id_type=MESH)
    for i in range(NB):

        @pl.when(jnp.logical_not(is_self(i)))
        def _():
            pl.semaphore_signal(barrier, inc=1, device_id=peer(i), device_id_type=MESH)

    @pl.when(c == half)
    def _():
        pl.semaphore_wait(barrier, 6)

    @pl.when(c != half)
    def _():
        pl.semaphore_wait(barrier, 7)

    def remote(src, dst, ssem, rsem, dev):
        return pltpu.make_async_remote_copy(
            src_ref=src, dst_ref=dst, send_sem=ssem, recv_sem=rsem, device_id=dev, device_id_type=MESH
        )

    def rows(i, n=T):
        return pl.ds(pl.multiple_of(i * n, n), n)

    def send_peer(i, src, dst, ssem, rsem):
        @pl.when(jnp.logical_not(is_self(i)))
        def _():
            remote(src, dst, ssem, rsem, peer(i)).start()

        @pl.when(is_self(i))
        def _():
            pltpu.make_async_copy(src, dst, rsem).start()

    def sent_peer(i, src, dst, ssem, rsem):
        @pl.when(jnp.logical_not(is_self(i)))
        def _():
            remote(src, dst, ssem, rsem, peer(i)).wait_send()

    def arrived(dst, rsem):
        pltpu.make_async_copy(dst, dst, rsem).wait()

    w_copy = pltpu.make_async_copy(w_hbm, wbuf, w_sem)
    w_copy.start()

    def in_args(a, i):
        src = (k_ref, v_ref, q_ref, doloc)[a].at[:, pl.ds(i * HD, HD)]
        if a < 2:
            dst = (kbuf, vbuf)[a].at[rows(NB + zi)]
        else:
            dst = (qbuf, dobuf)[a - 2].at[rows(zi)]
        return i, src, dst, in_send.at[a, i], in_recv.at[a, zi]

    def in_dst(a, j):
        if a < 2:
            return (kbuf, vbuf)[a].at[rows(NB + j)], in_recv.at[a, j]
        return (qbuf, dobuf)[a - 2].at[rows(j)], in_recv.at[a, j]

    for i in range(NB):
        send_peer(*in_args(0, i))
    def cot_rows(g):
        return cotbuf.at[rows(g, ROWS)]

    cot_x = remote(cot_ref, cot_rows(h), cot_send.at[0], cot_recv.at[0], across)
    cot_s = remote(cot_ref, cot_rows(h), cot_send.at[1], cot_recv.at[1], sib)
    cot_x.start()
    cot_s.start()
    for a in (1, 2):
        for i in range(NB):
            send_peer(*in_args(a, i))
    cotbuf[rows(h, ROWS), :] = cot_ref[...]

    lens = len_ref[...].astype(F32)
    d_i = lax.broadcasted_iota(jnp.int32, (128, 128), 0)
    e_i = lax.broadcasted_iota(jnp.int32, (128, 128), 1)
    starts = jnp.sum(jnp.where(e_i < d_i, jnp.broadcast_to(lens, (128, 128)), 0.0), axis=1, keepdims=True)
    first = (base + NB * c) * T
    pos = (first + lax.broadcasted_iota(jnp.int32, (128, NB * T), 1)).astype(F32)
    started = jnp.where(jnp.broadcast_to(starts, (128, NB * T)) <= pos, starts, 0.0)
    low = jnp.max(started, axis=0, keepdims=True).astype(jnp.int32) - (first - NB * T)
    lo[...] = jnp.broadcast_to(low, (8, NB * T))
    dkacc[...] = jnp.zeros_like(dkacc)
    dvacc[...] = jnp.zeros_like(dvacc)

    def halo(a, j):
        buf = (kbuf, vbuf)[a]
        return remote(buf.at[rows(NB + j)], buf.at[rows(j)], halo_send.at[a, j], halo_recv.at[a, j], h_next)

    cot_f = remote(
        cot_rows(across[1]), cot_rows(across[1]), cot_send.at[2], cot_recv.at[2], sib
    )
    for j in range(NB):
        arrived(*in_dst(0, j))
        halo(0, j).start()
    arrived(cot_rows(across[1]), cot_recv.at[0])
    cot_f.start()
    for j in range(NB):
        arrived(*in_dst(1, j))
        halo(1, j).start()

    w_copy.wait()
    arrived(cot_rows(sib[1]), cot_recv.at[1])
    arrived(cot_rows(lax.rem(sib[1] + 2, 4)), cot_recv.at[2])
    doloc[...] = nt(cotbuf[...], wbuf[...]).astype(BF)
    for i in range(NB):
        send_peer(*in_args(3, i))

    for a in range(2):
        for j in range(NB):
            arrived((kbuf, vbuf)[a].at[rows(j)], halo_recv.at[a, j])
    for b in range(2 * NB):
        kT[:, b * T : (b + 1) * T] = kbuf[b * T : (b + 1) * T, :].T
        vT[:, b * T : (b + 1) * T] = vbuf[b * T : (b + 1) * T, :].T
    for j in range(NB):
        arrived(*in_dst(2, j))

    r_i = lax.broadcasted_iota(jnp.int32, (T, T), 0)
    t_i = lax.broadcasted_iota(jnp.int32, (T, T), 1)

    def out_args(a, i):
        src = (oout, dqout, dvout, dkout)[a].at[rows(i)]
        dst = (oin, dq_ref, dv_ref, dk_ref)[a].at[:, rows(zi, HD)]
        return i, src, dst, out_send.at[a, i], out_recv.at[a, zi]

    def out_dst(a, j):
        return (oin, dq_ref, dv_ref, dk_ref)[a].at[:, rows(j, HD)], out_recv.at[a, j]

    @pl.loop(0, NB)
    def _(i):
        q = qbuf[rows(i), :]
        low = lo[0:1, rows(i)] - i * T
        top = None
        for b in range(WIN):
            scores = nt(kbuf[rows(i + b), :], q)
            seen = r_i + b * T >= low
            if b == WIN - 1:
                seen = seen & (r_i <= t_i)
            scores = jnp.where(seen, scores, NEG)
            sbuf[b * T : (b + 1) * T, :] = scores
            part = fold(scores, jnp.maximum)
            top = part if top is None else jnp.maximum(top, part)
        top = jnp.max(top, axis=0, keepdims=True) * SCALE
        total = None
        att = None
        for b in range(WIN):
            p = jnp.exp2(sbuf[b * T : (b + 1) * T, :] * SCALE - top)
            part = fold(p, jnp.add)
            total = part if total is None else total + part
            pb = p.astype(BF)
            pbuf[rows(i * WIN + b), :] = pb
            term = nn(vT[:, rows(i + b)], pb)
            att = term if att is None else att + term
        inv = 1.0 / jnp.sum(total, axis=0, keepdims=True)
        linv[rows(i, 8), :] = jnp.broadcast_to(inv, (8, T))
        att = (att * inv).astype(BF)
        oT[rows(i, HD), :] = att
        oout[rows(i), :] = att.T
        send_peer(*out_args(0, i))

    for j in range(NB):
        arrived(*in_dst(3, j))

    def back(a, u):
        src, dst = ((hvo, hvi), (hko, hki))[a]
        return remote(src.at[rows(u)], dst.at[rows(u)], hg_send.at[a, u], hg_recv.at[a, u], h_prev)

    @pl.loop(0, NB)
    def _(i):
        q = qbuf[rows(i), :]
        inv = linv[rows(i, 8), :][0:1]
        doT = dobuf[rows(i), :].astype(F32).T * inv
        delta = jnp.sum(doT * oT[rows(i, HD), :].astype(F32), axis=0, keepdims=True)
        doT = doT.astype(BF)
        do = doT.T
        gq = None
        for b in range(WIN):
            pb = pbuf[rows(i * WIN + b), :]
            dvacc[rows(i + b), :] += nn(pb, do)
            dp = nn(vbuf[rows(i + b), :], doT)
            ds = (pb.astype(F32) * (dp - delta)).astype(BF)
            term = nn(kT[:, rows(i + b)], ds)
            gq = term if gq is None else gq + term
            dkacc[rows(i + b), :] += nn(ds, q)
        dqout[rows(i), :] = (gq * FACTOR).astype(BF).T
        send_peer(*out_args(1, i))
        hvo[rows(i), :] = dvacc[rows(i), :].astype(BF)
        back(0, i).start()
        hko[rows(i), :] = dkacc[rows(i), :].astype(BF)
        back(1, i).start()

    for j in range(NB):
        arrived(*out_dst(0, j))

    def o_rows(first_row):
        return oin[rows(first_row, ROWS), :]

    other = jnp.concatenate([o_rows(1 - c), o_rows(3 - c)], axis=0)
    pa_out[...] = nn(other, wbuf[...]).astype(BF)
    pr_a = remote(pa_out, pa_in, pr_send.at[0], pr_recv.at[0], sib)
    pr_a.start()

    for u in range(NB):
        arrived(hvi.at[rows(u)], hg_recv.at[0, u])
        dvout[rows(u), :] = (dvacc[rows(NB + u), :] + hvi[rows(u), :].astype(F32)).astype(BF)
        send_peer(*out_args(2, u))

    far = nn(o_rows(c + 2 * (1 - yl)), wbuf[...])
    arrived(pa_in, pr_recv.at[0])
    pb_out[...] = (far + pa_in[rows(1 - yl, ROWS), :].astype(F32)).astype(BF)
    pr_b = remote(pb_out, pb_in, pr_send.at[1], pr_recv.at[1], across)
    pr_b.start()
    near = nn(o_rows(h), wbuf[...]) + pa_in[rows(yl, ROWS), :].astype(F32)

    for u in range(NB):
        arrived(hki.at[rows(u)], hg_recv.at[1, u])
        own = dkacc[rows(NB + u), :] + hki[rows(u), :].astype(F32)
        dkout[rows(u), :] = (own * FACTOR).astype(BF)
        send_peer(*out_args(3, u))

    arrived(pb_in, pr_recv.at[1])
    proj_ref[...] = (near + pb_in[...].astype(F32)).astype(BF)

    for a in range(1, 4):
        for j in range(NB):
            arrived(*out_dst(a, j))

    for a in range(4):
        for i in range(NB):
            sent_peer(*in_args(a, i))
            sent_peer(*out_args(a, i))
    for a in range(2):
        for j in range(NB):
            halo(a, j).wait_send()
            back(a, j).wait_send()
    for copy in (cot_x, cot_s, cot_f, pr_a, pr_b):
        copy.wait_send()


def per_device(seq_size, queries, keys, values, out_weight, cotangent, doc_lengths):
    flat = [x.reshape(T, NB * HD) for x in (queries, keys, values)]
    vmem = pl.BlockSpec(memory_space=pltpu.VMEM)

    def sc(*shape, dtype=BF):
        return pltpu.VMEM(shape, dtype)

    dma = pltpu.SemaphoreType.DMA
    half = NB * T
    proj, dq, dk, dv = pl.pallas_call(
        functools.partial(kernel, seq_size),
        out_shape=[jax.ShapeDtypeStruct((ROWS, D), BF)]
        + [jax.ShapeDtypeStruct((T, NB * HD), BF)] * 3,
        in_specs=[vmem, vmem, vmem, pl.BlockSpec(memory_space=pl.ANY), vmem, vmem],
        out_specs=[vmem] * 4,
        scratch_shapes=[
            sc(2 * half, HD),
            sc(2 * half, HD),
            sc(half, HD),
            sc(half, HD),
            sc(HD, 2 * half),
            sc(HD, 2 * half),
            sc(T, D),
            sc(NB * HD, D),
            sc(T, NB * HD),
            sc(WIN * T, T, dtype=F32),
            sc(NB * WIN * T, T),
            sc(NB * HD, T),
            sc(NB * 8, T, dtype=F32),
            sc(8, half, dtype=jnp.int32),
            sc(2 * half, HD, dtype=F32),
            sc(2 * half, HD, dtype=F32),
            sc(half, HD),
            sc(half, HD),
            sc(half, HD),
            sc(half, HD),
            sc(half, HD),
            sc(half, HD),
            sc(half, HD),
            sc(half, HD),
            sc(T, NB * HD),
            sc(2 * ROWS, D),
            sc(2 * ROWS, D),
            sc(ROWS, D),
            sc(ROWS, D),
            dma((4, NB)),
            dma((4, NB)),
            dma((2, NB)),
            dma((2, NB)),
            dma((3,)),
            dma((3,)),
            dma((4, NB)),
            dma((4, NB)),
            dma((2, NB)),
            dma((2, NB)),
            dma((2,)),
            dma((2,)),
            dma(()),
        ],
        compiler_params=pltpu.CompilerParams(
            collective_id=0, has_side_effects=True, vmem_limit_bytes=48 * 1024 * 1024
        ),
        name="ring_attention",
    )(*flat, out_weight, cotangent, doc_lengths.reshape(1, -1))
    return (proj,) + tuple(x.reshape(T, NB, HD) for x in (dq, dk, dv))


def solution(mesh):
    seq_head = P("seq", "head", None)
    rows = P(("seq", "head"), None)
    return jax.shard_map(
        functools.partial(per_device, mesh.shape["seq"]),
        mesh=mesh,
        in_specs=(seq_head, seq_head, seq_head, P("head", None), rows, P()),
        out_specs=(rows, seq_head, seq_head, seq_head),
        check_vma=False,
    )
```

time: 281 us -> 74.8 us (0.27)
  the two profiles are of different devices: /device:TPU:30 before, /device:TPU:1 now
where the time goes in v1:
time: 74.8 us; the launch traced here: 74.5 us
  Pallas kernels  65.6 us (88%)
  local copies, waits for them, and re-layouts  8.28 us (11%)
    pallas_call x1, Pallas kernels, per_device(): pl.pallas_call(functools.partial(kernel, seq_size), out_shape=[jax.ShapeD...  65.6 us
    unnamed x8, local copies, waits for them, and re-layouts  4.88 us
    reshape x3, local copies, waits for them, and re-layouts, per_device(): return (proj,) + tuple((x.reshape(T, NB, HD) for x in (dq, dk, dv)))  2.3 us

profile of v1, /device:TPU:1, one launch (start us, length us, event | category | flops | bytes accessed | tf_op | source)
XLA Modules:
  0.0 74.5 jit_solution(13400275559604420504)
XLA Ops:
  0.6 1.0 %copy.16 = bf16[32,8,4,128]{3,1,2,0:T(8,128)(2,1)S(1)} copy(bf16[32,8,4,128]{3,2,1,0:T(4,128)(2,1)} %bitcast.13) | data formatting | bytes 524288
  1.6 1.1 %copy_bitcast_fusion = (bf16[256,512]{1,0:T(8,128)(2,1)S(1)}, bf16[256,512]{1,0:T(8,128)(2,1)S(1)}) fusion(bf16[32,8,4,128]{3,2,1,0:T(4,128)(2,1)} %bitcast.14, bf16[32,8,4,128]{3,2,1,0:T(4,128)(2,1)} %bitcast.15), kind=kLoop, calls=%fused_computation | loop fusion | bytes 1048576 | tf_op jit(solution)/shard_map/reshape | solution.py:358
  2.7 0.0 copy-start
  2.7 1.6 %copy-done = bf16[512,2048]{1,0:T(8,128)(2,1)S(1)} copy-done((bf16[512,2048]{1,0:T(8,128)(2,1)S(1)}, bf16[512,2048]{1,0:T(8,128)(2,1)}, u32[]{:S(2)}) %copy-start) | copy-done | bytes 2097176
  4.3 0.0 copy-start.1
  4.3 0.9 %copy-done.1 = bf16[64,2048]{1,0:T(8,128)(2,1)S(1)} copy-done((bf16[64,2048]{1,0:T(8,128)(2,1)S(1)}, bf16[64,2048]{1,0:T(8,128)(2,1)}, u32[]{:S(2)}) %copy-start.1) | copy-done | bytes 262168
  5.3 0.0 copy-start.2
  5.3 0.7 copy-done.2
  5.9 65.6 %ring_attention.1 = (bf16[64,2048]{1,0:T(8,128)(2,1)S(1)}, bf16[256,512]{1,0:T(8,128)(2,1)S(1)}, bf16[256,512]{1,0:T(8,128)(2,1)S(1)}, bf16[256,512]{1,0:T(8,128)(2,1)S(1)}) custom-call(bf16[256,512]{1,0:T(8,128)(2,1)S(1)} %bitcast.11, bf16[256,512]{1,0:T(8,128)(2,1)S(1)} %get-tuple-element.13.k_ref, bf16[256,512]{1,0:T(8,128)(2,1)S(1)} %get-tuple-element.12.v_ref, ...), custom_call_target="tpu_custom_call" | custom-call | tf_op jit(solution)/shard_map/ring_attention/pallas_call | solution.py:366
  71.5 0.8 %reshape.33 = bf16[256,4,128]{2,1,0:T(4,128)(2,1)} reshape(bf16[256,512]{1,0:T(8,128)(2,1)S(1)} %get-tuple-element.9) | data formatting | bytes 524288 | tf_op jit(solution)/shard_map/reshape | solution.py:421
  72.3 0.8 %reshape.34 = bf16[256,4,128]{2,1,0:T(4,128)(2,1)} reshape(bf16[256,512]{1,0:T(8,128)(2,1)S(1)} %get-tuple-element.10) | data formatting | bytes 524288 | tf_op jit(solution)/shard_map/reshape | solution.py:421
  73.1 0.8 %reshape.35 = bf16[256,4,128]{2,1,0:T(4,128)(2,1)} reshape(bf16[256,512]{1,0:T(8,128)(2,1)S(1)} %get-tuple-element.11) | data formatting | bytes 524288 | tf_op jit(solution)/shard_map/reshape | solution.py:421
  73.8 0.7 copy.18
Async XLA Ops:
  2.7 1.6 %copy-start = (bf16[512,2048]{1,0:T(8,128)(2,1)S(1)}, bf16[512,2048]{1,0:T(8,128)(2,1)}, u32[]{:S(2)}) copy-start(bf16[512,2048]{1,0:T(8,128)(2,1)} %w_hbm.1) | copy-start | bytes 6291460
  4.3 0.9 %copy-start.1 = (bf16[64,2048]{1,0:T(8,128)(2,1)S(1)}, bf16[64,2048]{1,0:T(8,128)(2,1)}, u32[]{:S(2)}) copy-start(bf16[64,2048]{1,0:T(8,128)(2,1)} %cot_ref.1) | copy-start | bytes 786436
  5.3 0.7 copy-start.2

commit v2 on v1

--- a/solution.py
+++ b/solution.py
@@ -43,12 +43,12 @@
 
 def kernel(
     seq_size,
-    q_ref,
-    k_ref,
-    v_ref,
+    q_hbm,
+    k_hbm,
+    v_hbm,
     w_hbm,
-    cot_ref,
-    len_ref,
+    cot_hbm,
+    len_hbm,
     proj_ref,
     dq_ref,
     dk_ref,
@@ -77,7 +77,18 @@
     dqout,
     dkout,
     dvout,
+    k_ref,
+    v_ref,
+    q_ref,
+    cot_ref,
+    len_ref,
+    kloc,
+    vloc,
+    qloc,
     oin,
+    dqin,
+    dvin,
+    dkin,
     pa_out,
     pa_in,
     pb_out,
@@ -116,6 +127,22 @@
     def is_self(i):
         return (c == half) & (zi == i)
 
+    loads = [
+        pltpu.make_async_copy(src, dst, w_sem.at[n])
+        for n, (src, dst) in enumerate(
+            (
+                (k_hbm, k_ref),
+                (v_hbm, v_ref),
+                (q_hbm, q_ref),
+                (cot_hbm, cot_ref),
+                (len_hbm, len_ref),
+                (w_hbm, wbuf),
+            )
+        )
+    ]
+    for copy in loads:
+        copy.start()
+
     barrier = pltpu.get_barrier_semaphore()
     for dev in (sib, across, ring_adj):
         pl.semaphore_signal(barrier, inc=1, device_id=dev, device_id_type=MESH)
@@ -125,14 +152,6 @@
         def _():
             pl.semaphore_signal(barrier, inc=1, device_id=peer(i), device_id_type=MESH)
 
-    @pl.when(c == half)
-    def _():
-        pl.semaphore_wait(barrier, 6)
-
-    @pl.when(c != half)
-    def _():
-        pl.semaphore_wait(barrier, 7)
-
     def remote(src, dst, ssem, rsem, dev):
         return pltpu.make_async_remote_copy(
             src_ref=src, dst_ref=dst, send_sem=ssem, recv_sem=rsem, device_id=dev, device_id_type=MESH
@@ -158,11 +177,13 @@
     def arrived(dst, rsem):
         pltpu.make_async_copy(dst, dst, rsem).wait()
 
-    w_copy = pltpu.make_async_copy(w_hbm, wbuf, w_sem)
-    w_copy.start()
+    def split(src, dst):
+        for i in range(NB):
+            dst[i * T : (i + 1) * T, :] = src[:, i, :]
+
 
     def in_args(a, i):
-        src = (k_ref, v_ref, q_ref, doloc)[a].at[:, pl.ds(i * HD, HD)]
+        src = (kloc, vloc, qloc, doloc)[a].at[rows(i)]
         if a < 2:
             dst = (kbuf, vbuf)[a].at[rows(NB + zi)]
         else:
@@ -174,6 +195,17 @@
             return (kbuf, vbuf)[a].at[rows(NB + j)], in_recv.at[a, j]
         return (qbuf, dobuf)[a - 2].at[rows(j)], in_recv.at[a, j]
 
+    loads[0].wait()
+    split(k_ref, kloc)
+    loads[3].wait()
+    @pl.when(c == half)
+    def _():
+        pl.semaphore_wait(barrier, 6)
+
+    @pl.when(c != half)
+    def _():
+        pl.semaphore_wait(barrier, 7)
+
     for i in range(NB):
         send_peer(*in_args(0, i))
     def cot_rows(g):
@@ -184,10 +216,13 @@
     cot_x.start()
     cot_s.start()
     for a in (1, 2):
+        loads[a].wait()
+        split((k_ref, v_ref, q_ref)[a], (kloc, vloc, qloc)[a])
         for i in range(NB):
             send_peer(*in_args(a, i))
     cotbuf[rows(h, ROWS), :] = cot_ref[...]
 
+    loads[4].wait()
     lens = len_ref[...].astype(F32)
     d_i = lax.broadcasted_iota(jnp.int32, (128, 128), 0)
     e_i = lax.broadcasted_iota(jnp.int32, (128, 128), 1)
@@ -216,11 +251,12 @@
         arrived(*in_dst(1, j))
         halo(1, j).start()
 
-    w_copy.wait()
+    loads[5].wait()
     arrived(cot_rows(sib[1]), cot_recv.at[1])
     arrived(cot_rows(lax.rem(sib[1] + 2, 4)), cot_recv.at[2])
-    doloc[...] = nt(cotbuf[...], wbuf[...]).astype(BF)
+    d_att = nt(cotbuf[...], wbuf[...]).astype(BF)
     for i in range(NB):
+        doloc[i * T : (i + 1) * T, :] = d_att[:, i * HD : (i + 1) * HD]
         send_peer(*in_args(3, i))
 
     for a in range(2):
@@ -237,11 +273,11 @@
 
     def out_args(a, i):
         src = (oout, dqout, dvout, dkout)[a].at[rows(i)]
-        dst = (oin, dq_ref, dv_ref, dk_ref)[a].at[:, rows(zi, HD)]
+        dst = (oin, dqin, dvin, dkin)[a].at[rows(zi)]
         return i, src, dst, out_send.at[a, i], out_recv.at[a, zi]
 
     def out_dst(a, j):
-        return (oin, dq_ref, dv_ref, dk_ref)[a].at[:, rows(j, HD)], out_recv.at[a, j]
+        return (oin, dqin, dvin, dkin)[a].at[rows(j)], out_recv.at[a, j]
 
     @pl.loop(0, NB)
     def _(i):
@@ -310,17 +346,15 @@
         arrived(*out_dst(0, j))
 
     def o_rows(first_row):
-        return oin[rows(first_row, ROWS), :]
+        return jnp.concatenate(
+            [oin[pl.ds(pl.multiple_of(j * T + first_row * ROWS, ROWS), ROWS), :] for j in range(NB)],
+            axis=1,
+        )
 
     other = jnp.concatenate([o_rows(1 - c), o_rows(3 - c)], axis=0)
     pa_out[...] = nn(other, wbuf[...]).astype(BF)
     pr_a = remote(pa_out, pa_in, pr_send.at[0], pr_recv.at[0], sib)
     pr_a.start()
-
-    for u in range(NB):
-        arrived(hvi.at[rows(u)], hg_recv.at[0, u])
-        dvout[rows(u), :] = (dvacc[rows(NB + u), :] + hvi[rows(u), :].astype(F32)).astype(BF)
-        send_peer(*out_args(2, u))
 
     far = nn(o_rows(c + 2 * (1 - yl)), wbuf[...])
     arrived(pa_in, pr_recv.at[0])
@@ -330,6 +364,9 @@
     near = nn(o_rows(h), wbuf[...]) + pa_in[rows(yl, ROWS), :].astype(F32)
 
     for u in range(NB):
+        arrived(hvi.at[rows(u)], hg_recv.at[0, u])
+        dvout[rows(u), :] = (dvacc[rows(NB + u), :] + hvi[rows(u), :].astype(F32)).astype(BF)
+        send_peer(*out_args(2, u))
         arrived(hki.at[rows(u)], hg_recv.at[1, u])
         own = dkacc[rows(NB + u), :] + hki[rows(u), :].astype(F32)
         dkout[rows(u), :] = (own * FACTOR).astype(BF)
@@ -341,6 +378,8 @@
     for a in range(1, 4):
         for j in range(NB):
             arrived(*out_dst(a, j))
+            src = (dqin, dvin, dkin)[a - 1]
+            (dq_ref, dv_ref, dk_ref)[a - 1][:, j, :] = src[j * T : (j + 1) * T, :]
 
     for a in range(4):
         for i in range(NB):
@@ -354,8 +393,13 @@
         copy.wait_send()
 
 
+def drain(*refs):
+    for n in range(4):
+        refs[4+n][...]=refs[n][...]
+
+
 def per_device(seq_size, queries, keys, values, out_weight, cotangent, doc_lengths):
-    flat = [x.reshape(T, NB * HD) for x in (queries, keys, values)]
+    hbm = pl.BlockSpec(memory_space=pltpu.HBM)
     vmem = pl.BlockSpec(memory_space=pltpu.VMEM)
 
     def sc(*shape, dtype=BF):
@@ -363,11 +407,11 @@
 
     dma = pltpu.SemaphoreType.DMA
     half = NB * T
-    proj, dq, dk, dv = pl.pallas_call(
+    results = pl.pallas_call(
         functools.partial(kernel, seq_size),
         out_shape=[jax.ShapeDtypeStruct((ROWS, D), BF)]
-        + [jax.ShapeDtypeStruct((T, NB * HD), BF)] * 3,
-        in_specs=[vmem, vmem, vmem, pl.BlockSpec(memory_space=pl.ANY), vmem, vmem],
+        + [jax.ShapeDtypeStruct((T, NB, HD), BF)] * 3,
+        in_specs=[hbm] * 6,
         out_specs=[vmem] * 4,
         scratch_shapes=[
             sc(2 * half, HD),
@@ -378,7 +422,7 @@
             sc(HD, 2 * half),
             sc(T, D),
             sc(NB * HD, D),
-            sc(T, NB * HD),
+            sc(half, HD),
             sc(WIN * T, T, dtype=F32),
             sc(NB * WIN * T, T),
             sc(NB * HD, T),
@@ -394,7 +438,18 @@
             sc(half, HD),
             sc(half, HD),
             sc(half, HD),
-            sc(T, NB * HD),
+            sc(T, NB, HD),
+            sc(T, NB, HD),
+            sc(T, NB, HD),
+            sc(ROWS, D),
+            sc(1, 128, dtype=jnp.int32),
+            sc(half, HD),
+            sc(half, HD),
+            sc(half, HD),
+            sc(half, HD),
+            sc(half, HD),
+            sc(half, HD),
+            sc(half, HD),
             sc(2 * ROWS, D),
             sc(2 * ROWS, D),
             sc(ROWS, D),
@@ -411,14 +466,20 @@
             dma((2, NB)),
             dma((2,)),
             dma((2,)),
-            dma(()),
+            dma((6,)),
         ],
         compiler_params=pltpu.CompilerParams(
-            collective_id=0, has_side_effects=True, vmem_limit_bytes=48 * 1024 * 1024
+            collective_id=0, has_side_effects=True, vmem_limit_bytes=60 * 1024 * 1024
         ),
         name="ring_attention",
-    )(*flat, out_weight, cotangent, doc_lengths.reshape(1, -1))
-    return (proj,) + tuple(x.reshape(T, NB, HD) for x in (dq, dk, dv))
+    )(queries, keys, values, out_weight, cotangent, doc_lengths.reshape(1, -1))
+    return pl.pallas_call(
+        drain,
+        out_shape=[jax.ShapeDtypeStruct(x.shape, x.dtype) for x in results],
+        in_specs=[vmem] * 4,
+        out_specs=[vmem] * 4,
+        name="drain",
+    )(*results)
 
 
 def solution(mesh):

time: 74.8 us -> 67.6 us (0.904)
  the two profiles are of different devices: /device:TPU:1 before, /device:TPU:64 now
where the time goes in v2:
time: 67.6 us; the launch traced here: 67.5 us
  Pallas kernels  66.8 us (99%)
    pallas_call x1, Pallas kernels, per_device(): pl.pallas_call(functools.partial(kernel, seq_size), out_shape=[jax.ShapeD...  64.6 us
    pallas_call x1, Pallas kernels, per_device(): pl.pallas_call(drain, out_shape=[jax.ShapeDtypeStruct(x.shape, x.dtype) f...  2.17 us

profile of v2, /device:TPU:64, one launch (start us, length us, event | category | flops | bytes accessed | tf_op | source)
XLA Modules:
  0.0 67.5 jit_solution(16891139172471990770)
XLA Ops:
  0.6 64.6 %ring_attention.1 = (bf16[64,2048]{1,0:T(8,128)(2,1)}, bf16[256,4,128]{2,1,0:T(4,128)(2,1)}, bf16[256,4,128]{2,1,0:T(4,128)(2,1)}, bf16[256,4,128]{2,1,0:T(4,128)(2,1)}) custom-call(bf16[256,4,128]{2,1,0:T(4,128)(2,1)} %q_hbm.1, bf16[256,4,128]{2,1,0:T(4,128)(2,1)} %k_hbm.1, bf16[256,4,128]{2,1,0:T(4,128)(2,1)} %v_hbm.1, bf16[512,2048]{1,0:T(8,128)(2,1)} %w_hbm.1, ...), custom_call_target="tpu_custom_call" | custom-call | tf_op jit(solution)/shard_map/ring_attention/pallas_call | solution.py:410
  65.3 2.2 %drain.1 = (bf16[64,2048]{1,0:T(8,128)(2,1)}, bf16[256,4,128]{2,1,0:T(4,128)(2,1)}, bf16[256,4,128]{2,1,0:T(4,128)(2,1)}, bf16[256,4,128]{2,1,0:T(4,128)(2,1)}) custom-call(bf16[64,2048]{1,0:T(8,128)(2,1)} %get-tuple-element.8.refs_0_, bf16[256,4,128]{2,1,0:T(4,128)(2,1)} %get-tuple-element.9.refs_1_, bf16[256,4,128]{2,1,0:T(4,128)(2,1)} %get-tuple-element.10.refs_2_, ...), custom_call_target="tpu_custom_call" | custom-call | tf_op jit(solution)/shard_map/drain/pallas_call | solution.py:476

commit v3 on v2

--- a/solution.py
+++ b/solution.py
@@ -49,10 +49,10 @@
     w_hbm,
     cot_hbm,
     len_hbm,
-    proj_ref,
-    dq_ref,
-    dk_ref,
-    dv_ref,
+    proj_hbm,
+    dq_hbm,
+    dk_hbm,
+    dv_hbm,
     kbuf,
     vbuf,
     qbuf,
@@ -66,6 +66,8 @@
     pbuf,
     oT,
     linv,
+    doT,
+    deltas,
     lo,
     dkacc,
     dvacc,
@@ -77,6 +79,10 @@
     dqout,
     dkout,
     dvout,
+    proj_ref,
+    dq_ref,
+    dk_ref,
+    dv_ref,
     k_ref,
     v_ref,
     q_ref,
@@ -106,6 +112,7 @@
     pr_send,
     pr_recv,
     w_sem,
+    r_sem,
 ):
     s = lax.axis_index("seq")
     h = lax.axis_index("head")
@@ -121,6 +128,10 @@
     h_prev = (lax.rem(s + seq_size - RING * (1 - c), seq_size), h + 1 - 2 * c)
     ring_adj = (lax.rem(s + seq_size + RING * (2 * c - 1), seq_size), h + 1 - 2 * c)
 
+    no_halo_in = (s < RING) & (c == 0)
+    no_halo_out = (s >= seq_size - RING) & (c == 1)
+    alone = no_halo_in | no_halo_out
+
     def peer(i):
         return (base + NB * c + i, h - c + half)
 
@@ -140,12 +151,17 @@
             )
         )
     ]
-    for copy in loads:
+    for copy in loads[:5]:
         copy.start()
 
     barrier = pltpu.get_barrier_semaphore()
-    for dev in (sib, across, ring_adj):
+    for dev in (sib, across):
         pl.semaphore_signal(barrier, inc=1, device_id=dev, device_id_type=MESH)
+
+    @pl.when(jnp.logical_not(alone))
+    def _():
+        pl.semaphore_signal(barrier, inc=1, device_id=ring_adj, device_id_type=MESH)
+
     for i in range(NB):
 
         @pl.when(jnp.logical_not(is_self(i)))
@@ -177,9 +193,8 @@
     def arrived(dst, rsem):
         pltpu.make_async_copy(dst, dst, rsem).wait()
 
-    def split(src, dst):
-        for i in range(NB):
-            dst[i * T : (i + 1) * T, :] = src[:, i, :]
+    def split(src, dst, i):
+        dst[i * T : (i + 1) * T, :] = src[:, i, :]
 
 
     def in_args(a, i):
@@ -196,15 +211,11 @@
         return (qbuf, dobuf)[a - 2].at[rows(j)], in_recv.at[a, j]
 
     loads[0].wait()
-    split(k_ref, kloc)
+    loads[5].start()
+    for i in range(NB):
+        split(k_ref, kloc, i)
     loads[3].wait()
-    @pl.when(c == half)
-    def _():
-        pl.semaphore_wait(barrier, 6)
-
-    @pl.when(c != half)
-    def _():
-        pl.semaphore_wait(barrier, 7)
+    pl.semaphore_wait(barrier, 5 + jnp.where(c != half, 1, 0) + jnp.where(alone, 0, 1))
 
     for i in range(NB):
         send_peer(*in_args(0, i))
@@ -217,9 +228,8 @@
     cot_s.start()
     for a in (1, 2):
         loads[a].wait()
-        split((k_ref, v_ref, q_ref)[a], (kloc, vloc, qloc)[a])
         for i in range(NB):
-            send_peer(*in_args(a, i))
+            split((k_ref, v_ref, q_ref)[a], (kloc, vloc, qloc)[a], i)
     cotbuf[rows(h, ROWS), :] = cot_ref[...]
 
     loads[4].wait()
@@ -232,6 +242,16 @@
     started = jnp.where(jnp.broadcast_to(starts, (128, NB * T)) <= pos, starts, 0.0)
     low = jnp.max(started, axis=0, keepdims=True).astype(jnp.int32) - (first - NB * T)
     lo[...] = jnp.broadcast_to(low, (8, NB * T))
+    @pl.when(no_halo_in)
+    def _():
+        for buf in (kbuf, vbuf):
+            buf[0 : NB * T, :] = jnp.zeros((NB * T, HD), BF)
+
+    @pl.when(no_halo_out)
+    def _():
+        for buf in (hki, hvi):
+            buf[...] = jnp.zeros_like(buf)
+
     dkacc[...] = jnp.zeros_like(dkacc)
     dvacc[...] = jnp.zeros_like(dvacc)
 
@@ -242,14 +262,17 @@
     cot_f = remote(
         cot_rows(across[1]), cot_rows(across[1]), cot_send.at[2], cot_recv.at[2], sib
     )
+    for i in range(NB):
+        sent_peer(*in_args(0, i))
+    for i in range(NB):
+        send_peer(*in_args(1, i))
+    for i in range(NB):
+        send_peer(*in_args(2, i))
     for j in range(NB):
         arrived(*in_dst(0, j))
-        halo(0, j).start()
+        pl.when(jnp.logical_not(no_halo_out))(halo(0, j).start)
     arrived(cot_rows(across[1]), cot_recv.at[0])
     cot_f.start()
-    for j in range(NB):
-        arrived(*in_dst(1, j))
-        halo(1, j).start()
 
     loads[5].wait()
     arrived(cot_rows(sib[1]), cot_recv.at[1])
@@ -259,9 +282,16 @@
         doloc[i * T : (i + 1) * T, :] = d_att[:, i * HD : (i + 1) * HD]
         send_peer(*in_args(3, i))
 
-    for a in range(2):
-        for j in range(NB):
-            arrived((kbuf, vbuf)[a].at[rows(j)], halo_recv.at[a, j])
+    for j in range(NB):
+        arrived(*in_dst(1, j))
+        pl.when(jnp.logical_not(no_halo_out))(halo(1, j).start)
+
+    @pl.when(jnp.logical_not(no_halo_in))
+    def _():
+        for a in range(2):
+            for j in range(NB):
+                arrived((kbuf, vbuf)[a].at[rows(j)], halo_recv.at[a, j])
+
     for b in range(2 * NB):
         kT[:, b * T : (b + 1) * T] = kbuf[b * T : (b + 1) * T, :].T
         vT[:, b * T : (b + 1) * T] = vbuf[b * T : (b + 1) * T, :].T
@@ -320,27 +350,35 @@
 
     @pl.loop(0, NB)
     def _(i):
+        inv = linv[rows(i, 8), :][0:1]
+        scaled = dobuf[rows(i), :].astype(F32).T * inv
+        delta = jnp.sum(scaled * oT[rows(i, HD), :].astype(F32), axis=0, keepdims=True)
+        deltas[rows(i, 8), :] = jnp.broadcast_to(delta, (8, T))
+        scaled = scaled.astype(BF)
+        doT[rows(i, HD), :] = scaled
+        do = scaled.T
+        for b in range(WIN):
+            dvacc[rows(i + b), :] += nn(pbuf[rows(i * WIN + b), :], do)
+        hvo[rows(i), :] = dvacc[rows(i), :].astype(BF)
+        pl.when(jnp.logical_not(no_halo_in))(back(0, i).start)
+
+    @pl.loop(0, NB)
+    def _(i):
         q = qbuf[rows(i), :]
-        inv = linv[rows(i, 8), :][0:1]
-        doT = dobuf[rows(i), :].astype(F32).T * inv
-        delta = jnp.sum(doT * oT[rows(i, HD), :].astype(F32), axis=0, keepdims=True)
-        doT = doT.astype(BF)
-        do = doT.T
+        delta = deltas[rows(i, 8), :][0:1]
+        scaled = doT[rows(i, HD), :]
         gq = None
         for b in range(WIN):
             pb = pbuf[rows(i * WIN + b), :]
-            dvacc[rows(i + b), :] += nn(pb, do)
-            dp = nn(vbuf[rows(i + b), :], doT)
+            dp = nn(vbuf[rows(i + b), :], scaled)
             ds = (pb.astype(F32) * (dp - delta)).astype(BF)
             term = nn(kT[:, rows(i + b)], ds)
             gq = term if gq is None else gq + term
             dkacc[rows(i + b), :] += nn(ds, q)
+        hko[rows(i), :] = dkacc[rows(i), :].astype(BF)
+        pl.when(jnp.logical_not(no_halo_in))(back(1, i).start)
         dqout[rows(i), :] = (gq * FACTOR).astype(BF).T
         send_peer(*out_args(1, i))
-        hvo[rows(i), :] = dvacc[rows(i), :].astype(BF)
-        back(0, i).start()
-        hko[rows(i), :] = dkacc[rows(i), :].astype(BF)
-        back(1, i).start()
 
     for j in range(NB):
         arrived(*out_dst(0, j))
@@ -364,43 +402,70 @@
     near = nn(o_rows(h), wbuf[...]) + pa_in[rows(yl, ROWS), :].astype(F32)
 
     for u in range(NB):
-        arrived(hvi.at[rows(u)], hg_recv.at[0, u])
+
+        @pl.when(jnp.logical_not(no_halo_out))
+        def _():
+            arrived(hvi.at[rows(u)], hg_recv.at[0, u])
+
         dvout[rows(u), :] = (dvacc[rows(NB + u), :] + hvi[rows(u), :].astype(F32)).astype(BF)
         send_peer(*out_args(2, u))
-        arrived(hki.at[rows(u)], hg_recv.at[1, u])
+
+        @pl.when(jnp.logical_not(no_halo_out))
+        def _():
+            arrived(hki.at[rows(u)], hg_recv.at[1, u])
+
         own = dkacc[rows(NB + u), :] + hki[rows(u), :].astype(F32)
         dkout[rows(u), :] = (own * FACTOR).astype(BF)
         send_peer(*out_args(3, u))
 
     arrived(pb_in, pr_recv.at[1])
+    stores = [
+        pltpu.make_async_copy(src, dst, r_sem.at[n])
+        for n, (src, dst) in enumerate(
+            ((dq_ref, dq_hbm), (dv_ref, dv_hbm), (dk_ref, dk_hbm), (proj_ref, proj_hbm))
+        )
+    ]
     proj_ref[...] = (near + pb_in[...].astype(F32)).astype(BF)
+    stores[3].start()
 
     for a in range(1, 4):
         for j in range(NB):
             arrived(*out_dst(a, j))
             src = (dqin, dvin, dkin)[a - 1]
             (dq_ref, dv_ref, dk_ref)[a - 1][:, j, :] = src[j * T : (j + 1) * T, :]
+        stores[a - 1].start()
 
     for a in range(4):
         for i in range(NB):
-            sent_peer(*in_args(a, i))
+            if a > 0:
+                sent_peer(*in_args(a, i))
             sent_peer(*out_args(a, i))
     for a in range(2):
         for j in range(NB):
-            halo(a, j).wait_send()
-            back(a, j).wait_send()
+            pl.when(jnp.logical_not(no_halo_out))(halo(a, j).wait_send)
+            pl.when(jnp.logical_not(no_halo_in))(back(a, j).wait_send)
+    for copy in stores:
+        copy.wait()
     for copy in (cot_x, cot_s, cot_f, pr_a, pr_b):
         copy.wait_send()
 
 
 def drain(*refs):
+    src, dst, bufs = refs[:4], refs[4:8], refs[8:12]
+    r_sem, w_sem = refs[12:]
+    reads = [pltpu.make_async_copy(src[n], bufs[n], r_sem.at[n]) for n in range(4)]
+    writes = [pltpu.make_async_copy(bufs[n], dst[n], w_sem.at[n]) for n in range(4)]
+    for copy in reads:
+        copy.start()
     for n in range(4):
-        refs[4+n][...]=refs[n][...]
+        reads[n].wait()
+        writes[n].start()
+    for copy in writes:
+        copy.wait()
 
 
 def per_device(seq_size, queries, keys, values, out_weight, cotangent, doc_lengths):
     hbm = pl.BlockSpec(memory_space=pltpu.HBM)
-    vmem = pl.BlockSpec(memory_space=pltpu.VMEM)
 
     def sc(*shape, dtype=BF):
         return pltpu.VMEM(shape, dtype)
@@ -412,7 +477,7 @@
         out_shape=[jax.ShapeDtypeStruct((ROWS, D), BF)]
         + [jax.ShapeDtypeStruct((T, NB, HD), BF)] * 3,
         in_specs=[hbm] * 6,
-        out_specs=[vmem] * 4,
+        out_specs=[hbm] * 4,
         scratch_shapes=[
             sc(2 * half, HD),
             sc(2 * half, HD),
@@ -425,6 +490,8 @@
             sc(half, HD),
             sc(WIN * T, T, dtype=F32),
             sc(NB * WIN * T, T),
+            sc(NB * HD, T),
+            sc(NB * 8, T, dtype=F32),
             sc(NB * HD, T),
             sc(NB * 8, T, dtype=F32),
             sc(8, half, dtype=jnp.int32),
@@ -438,6 +505,10 @@
             sc(half, HD),
             sc(half, HD),
             sc(half, HD),
+            sc(ROWS, D),
+            sc(T, NB, HD),
+            sc(T, NB, HD),
+            sc(T, NB, HD),
             sc(T, NB, HD),
             sc(T, NB, HD),
             sc(T, NB, HD),
@@ -467,6 +538,7 @@
             dma((2,)),
             dma((2,)),
             dma((6,)),
+            dma((4,)),
         ],
         compiler_params=pltpu.CompilerParams(
             collective_id=0, has_side_effects=True, vmem_limit_bytes=60 * 1024 * 1024
@@ -476,8 +548,10 @@
     return pl.pallas_call(
         drain,
         out_shape=[jax.ShapeDtypeStruct(x.shape, x.dtype) for x in results],
-        in_specs=[vmem] * 4,
-        out_specs=[vmem] * 4,
+        in_specs=[pl.BlockSpec(memory_space=pl.ANY)] * 4,
+        out_specs=[hbm] * 4,
+        scratch_shapes=[sc(*x.shape) for x in results] + [dma((4,)), dma((4,))],
+        compiler_params=pltpu.CompilerParams(vmem_limit_bytes=60 * 1024 * 1024),
         name="drain",
     )(*results)
 

time: 67.6 us -> 66 us (0.976)
  the two profiles are of different devices: /device:TPU:64 before, /device:TPU:70 now
where the time goes in v3:
time: 66 us; the launch traced here: 65.8 us
  Pallas kernels  65.2 us (99%)
    pallas_call x1, Pallas kernels, per_device(): pl.pallas_call(functools.partial(kernel, seq_size), out_shape=[jax.ShapeD...  63.2 us
    pallas_call x1, Pallas kernels, per_device(): pl.pallas_call(drain, out_shape=[jax.ShapeDtypeStruct(x.shape, x.dtype) f...  1.98 us

profile of v3, /device:TPU:70, one launch (start us, length us, event | category | flops | bytes accessed | tf_op | source)
XLA Modules:
  0.0 65.8 jit_solution(10866606760376041826)
XLA Ops:
  0.6 63.2 %ring_attention.1 = (bf16[64,2048]{1,0:T(8,128)(2,1)}, bf16[256,4,128]{2,1,0:T(4,128)(2,1)}, bf16[256,4,128]{2,1,0:T(4,128)(2,1)}, bf16[256,4,128]{2,1,0:T(4,128)(2,1)}) custom-call(bf16[256,4,128]{2,1,0:T(4,128)(2,1)} %q_hbm.1, bf16[256,4,128]{2,1,0:T(4,128)(2,1)} %k_hbm.1, bf16[256,4,128]{2,1,0:T(4,128)(2,1)} %v_hbm.1, bf16[512,2048]{1,0:T(8,128)(2,1)} %w_hbm.1, ...), custom_call_target="tpu_custom_call" | custom-call | tf_op jit(solution)/shard_map/ring_attention/pallas_call | solution.py:475
  63.8 2.0 %drain.1 = (bf16[64,2048]{1,0:T(8,128)(2,1)}, bf16[256,4,128]{2,1,0:T(4,128)(2,1)}, bf16[256,4,128]{2,1,0:T(4,128)(2,1)}, bf16[256,4,128]{2,1,0:T(4,128)(2,1)}) custom-call(bf16[64,2048]{1,0:T(8,128)(2,1)} %get-tuple-element.8.refs_0_, bf16[256,4,128]{2,1,0:T(4,128)(2,1)} %get-tuple-element.9.refs_1_, bf16[256,4,128]{2,1,0:T(4,128)(2,1)} %get-tuple-element.10.refs_2_, ...), custom_call_target="tpu_custom_call" | custom-call | tf_op jit(solution)/shard_map/drain/pallas_call | solution.py:548

commit v4 on v3

--- a/solution.py
+++ b/solution.py
@@ -380,6 +380,26 @@
         dqout[rows(i), :] = (gq * FACTOR).astype(BF).T
         send_peer(*out_args(1, i))
 
+    def return_keys():
+        for u in range(NB):
+
+            @pl.when(jnp.logical_not(no_halo_out))
+            def _():
+                arrived(hvi.at[rows(u)], hg_recv.at[0, u])
+
+            dvout[rows(u), :] = (dvacc[rows(NB + u), :] + hvi[rows(u), :].astype(F32)).astype(BF)
+            send_peer(*out_args(2, u))
+
+            @pl.when(jnp.logical_not(no_halo_out))
+            def _():
+                arrived(hki.at[rows(u)], hg_recv.at[1, u])
+
+            own = dkacc[rows(NB + u), :] + hki[rows(u), :].astype(F32)
+            dkout[rows(u), :] = (own * FACTOR).astype(BF)
+            send_peer(*out_args(3, u))
+
+    pl.when(c == 0)(return_keys)
+
     for j in range(NB):
         arrived(*out_dst(0, j))
 
@@ -401,22 +421,7 @@
     pr_b.start()
     near = nn(o_rows(h), wbuf[...]) + pa_in[rows(yl, ROWS), :].astype(F32)
 
-    for u in range(NB):
-
-        @pl.when(jnp.logical_not(no_halo_out))
-        def _():
-            arrived(hvi.at[rows(u)], hg_recv.at[0, u])
-
-        dvout[rows(u), :] = (dvacc[rows(NB + u), :] + hvi[rows(u), :].astype(F32)).astype(BF)
-        send_peer(*out_args(2, u))
-
-        @pl.when(jnp.logical_not(no_halo_out))
-        def _():
-            arrived(hki.at[rows(u)], hg_recv.at[1, u])
-
-        own = dkacc[rows(NB + u), :] + hki[rows(u), :].astype(F32)
-        dkout[rows(u), :] = (own * FACTOR).astype(BF)
-        send_peer(*out_args(3, u))
+    pl.when(c == 1)(return_keys)
 
     arrived(pb_in, pr_recv.at[1])
     stores = [

time: 66 us -> 65.5 us (level)
  the two profiles are of different devices: /device:TPU:70 before, /device:TPU:15 now
where the time goes in v4:
time: 65.5 us; the launch traced here: 65.3 us
  Pallas kernels  64.7 us (99%)
    pallas_call x1, Pallas kernels, per_device(): pl.pallas_call(functools.partial(kernel, seq_size), out_shape=[jax.ShapeD...  62.7 us
    pallas_call x1, Pallas kernels, per_device(): pl.pallas_call(drain, out_shape=[jax.ShapeDtypeStruct(x.shape, x.dtype) f...  1.98 us

profile of v4, /device:TPU:15, one launch (start us, length us, event | category | flops | bytes accessed | tf_op | source)
XLA Modules:
  0.0 65.3 jit_solution(11362545710019975343)
XLA Ops:
  0.6 62.7 %ring_attention.1 = (bf16[64,2048]{1,0:T(8,128)(2,1)}, bf16[256,4,128]{2,1,0:T(4,128)(2,1)}, bf16[256,4,128]{2,1,0:T(4,128)(2,1)}, bf16[256,4,128]{2,1,0:T(4,128)(2,1)}) custom-call(bf16[256,4,128]{2,1,0:T(4,128)(2,1)} %q_hbm.1, bf16[256,4,128]{2,1,0:T(4,128)(2,1)} %k_hbm.1, bf16[256,4,128]{2,1,0:T(4,128)(2,1)} %v_hbm.1, bf16[512,2048]{1,0:T(8,128)(2,1)} %w_hbm.1, ...), custom_call_target="tpu_custom_call" | custom-call | tf_op jit(solution)/shard_map/ring_attention/pallas_call | solution.py:480
  63.3 2.0 %drain.1 = (bf16[64,2048]{1,0:T(8,128)(2,1)}, bf16[256,4,128]{2,1,0:T(4,128)(2,1)}, bf16[256,4,128]{2,1,0:T(4,128)(2,1)}, bf16[256,4,128]{2,1,0:T(4,128)(2,1)}) custom-call(bf16[64,2048]{1,0:T(8,128)(2,1)} %get-tuple-element.8.refs_0_, bf16[256,4,128]{2,1,0:T(4,128)(2,1)} %get-tuple-element.9.refs_1_, bf16[256,4,128]{2,1,0:T(4,128)(2,1)} %get-tuple-element.10.refs_2_, ...), custom_call_target="tpu_custom_call" | custom-call | tf_op jit(solution)/shard_map/drain/pallas_call | solution.py:553
